TPU v7x, 512 devices: a whole 4x4x16 slice. The times are simulated.
512 devices in a mesh: section: 8 (over x, core), tm: 64 (over y, z).
Axes of the slice: x: 4, y: 4, z: 16, core: 2. Of those that a mesh axis runs over, the one named last changes fastest.
Arguments:
- signal: bfloat16 [2, 16384, 128], P(None, 'tm'), may hold values from -6 to 6
- conv_weight: bfloat16 [8, 5, 384, 256], P('section'), may hold values from -0.3125 to 0.3125
- conv_bias: float32 [8, 5, 256], P('section'), may hold values from -3 to 3
- out_weight: bfloat16 [8, 5, 128, 256], P('section'), may hold values from -0.5 to 0.5
- out_bias: float32 [8, 5, 256], P('section'), may hold values from -3 to 3
Outputs:
- boundary_res: bfloat16 [8, 2, 16384, 128], P('section', None, 'tm')
- boundary_skip: float32 [8, 2, 16384, 128], P('section', None, 'tm')
All inputs are finite; a program needn't handle non-finite values.
Results may differ from a plain program's by a relative error of at most 0.028.
Values may be sent and summed in bfloat16 or wider, within the bound.
A program may use at most 64 MiB of HBM per device.

v0:
```python
import jax
import jax.numpy as jnp
from jax import lax
from jax.sharding import PartitionSpec as P

L_SECTION = 5


def passed_along(x, axis, by):
    peers = lax.axis_size(axis)
    pairs = [(i, i + by) for i in range(peers) if 0 <= i + by < peers]
    return lax.ppermute(x, axis, pairs)


def shards(signal, conv_weight, conv_bias, out_weight, out_bias):
    micro, rows, width = signal.shape
    sections = lax.axis_size("section")
    section = lax.axis_index("section")
    spans = (1, 16, rows // 4, rows // 2, 2 * rows)

    def apply_layer(inputs, layer):
        pre = (
            jnp.dot(inputs, conv_weight[0, layer], preferred_element_type=jnp.float32)
            + conv_bias[0, layer]
        )
        gated = (jnp.tanh(pre[:, :width]) * jax.nn.sigmoid(pre[:, width:])).astype(jnp.bfloat16)
        return (
            jnp.dot(gated, out_weight[0, layer], preferred_element_type=jnp.float32)
            + out_bias[0, layer]
        )

    def group_layers(entry, skip):
        state = entry.astype(jnp.float32)
        for layer in range(L_SECTION):
            inputs = state.astype(jnp.bfloat16)
            lag = spans[layer]
            if layer < L_SECTION - 1:
                border = passed_along(inputs[rows - 2 * lag :], "tm", 1)
                extended = jnp.concatenate([border, inputs], axis=0)
                back_two = extended[:rows]
                back_one = extended[lag : lag + rows]
            else:
                back_one = passed_along(inputs, "tm", 2)
                back_two = passed_along(inputs, "tm", 4)
            stacked = jnp.concatenate([back_two, back_one, inputs], axis=1)
            post = apply_layer(stacked, layer)
            state = state + post[:, :width]
            skip = skip + post[:, width:]
        return (state, skip)

    def advance(carry, tick):
        res_in, skip_in, res_buf, skip_buf = carry
        slot = tick - section
        valid = jnp.logical_and(slot >= 0, slot < micro)
        index = jnp.clip(slot, 0, micro - 1)
        first = section == 0
        fresh = lax.dynamic_index_in_dim(signal, index, 0, keepdims=False)
        entry = jnp.where(first, fresh, res_in)
        start = jnp.where(first, jnp.zeros_like(skip_in), skip_in)
        state, skip = group_layers(entry, start)
        res_out = state.astype(jnp.bfloat16)
        res_buf = jnp.where(
            valid, lax.dynamic_update_index_in_dim(res_buf, res_out, index, 0), res_buf
        )
        skip_buf = jnp.where(
            valid, lax.dynamic_update_index_in_dim(skip_buf, skip, index, 0), skip_buf
        )
        res_next, skip_next = (
            passed_along(res_out, "section", 1),
            passed_along(skip.astype(jnp.bfloat16), "section", 1).astype(skip.dtype),
        )
        return ((res_next, skip_next, res_buf, skip_buf), None)

    initial = (
        jnp.zeros((rows, width), jnp.bfloat16),
        jnp.zeros((rows, width), jnp.float32),
        jnp.zeros((micro, rows, width), jnp.bfloat16),
        jnp.zeros((micro, rows, width), jnp.float32),
    )
    ticks = jnp.arange(micro + sections - 1, dtype=jnp.int32)
    final, unused = lax.scan(advance, initial, ticks)
    res_buf = final[2]
    skip_buf = final[3]
    return (res_buf[None], skip_buf[None])


def solution(mesh):
    return jax.shard_map(
        shards,
        mesh=mesh,
        in_specs=(
            P(None, "tm", None),
            P("section", None, None, None),
            P("section", None, None),
            P("section", None, None, None),
            P("section", None, None),
        ),
        out_specs=(P("section", None, "tm", None), P("section", None, "tm", None)),
        check_vma=False,
    )
```

profile of v0, /device:TPU:30, one launch (start us, length us, event | category | flops | bytes accessed | tf_op | source)
XLA Modules:
  0.0 527.7 jit_solution(149556160718012241)
XLA Ops:
  1.7 525.3 %while.18 = (s32[]{:T(128)}, bf16[256,128]{1,0:T(8,128)(2,1)S(1)}, f32[256,128]{1,0:T(8,128)S(1)}, bf16[2,256,128]{2,1,0:T(8,128)(2,1)S(1)}, f32[2,256,128]{2,1,...) while((s32[]{:T(128)}, bf16[256,128]{1,0:T(8,128)(2,1)S(1)}, ...), condition=%wide.region_1.2_spmd.clone, body=%wide.region_0.1_spmd.clone.sunk | while | flops 342065152 | bytes 15764048 | solution.py:81
  6.7 9.2 %collective-permute-done = bf16[2,128]{1,0:T(2,128)(2,1)S(1)} collective-permute-done((bf16[2,128]{1,0:T(2,128)(2,1)S(1)}, bf16[2,128]{1,0:T(2,128)(2,1)S(1)}, u32[]{:S(2)}, u32[]{:S(2)}) %collective-permute-start) | collective-permute-done | bytes 544 | tf_op jit(solution)/shard_map/while/body/eval_jaxpr/ppermute | solution.py:12
  27.5 6.0 %collective-permute-done.2 = bf16[128,128]{1,0:T(8,128)(2,1)S(1)} collective-permute-done((bf16[128,128]{1,0:T(8,128)(2,1)S(1)}, bf16[128,128]{1,0:T(8,128)(2,1)S(1)}, u32[]{:S(2)}, u32[]{:S(2)}) %collective-permute-start.2) | collective-permute-done | bytes 32800 | tf_op jit(solution)/shard_map/while/body/eval_jaxpr/ppermute | solution.py:12
  35.9 6.3 %collective-permute-done.3 = bf16[256,128]{1,0:T(8,128)(2,1)S(1)} collective-permute-done((bf16[256,128]{1,0:T(8,128)(2,1)S(1)}, bf16[256,128]{1,0:T(8,128)(2,1)S(1)}, u32[]{:S(2)}, u32[]{:S(2)}) %collective-permute-start.3) | collective-permute-done | bytes 65568 | tf_op jit(solution)/shard_map/while/body/eval_jaxpr/ppermute | solution.py:12
  46.6 6.0 %collective-permute-done.4 = bf16[256,128]{1,0:T(8,128)(2,1)S(1)} collective-permute-done((bf16[256,128]{1,0:T(8,128)(2,1)S(1)}, bf16[256,128]{1,0:T(8,128)(2,1)S(1)}, u32[]{:S(2)}, u32[]{:S(2)}) %collective-permute-start.4) | collective-permute-done | bytes 65568 | tf_op jit(solution)/shard_map/while/body/eval_jaxpr/ppermute | solution.py:12
  84.7 6.0 %collective-permute-done.2 = bf16[128,128]{1,0:T(8,128)(2,1)S(1)} collective-permute-done((bf16[128,128]{1,0:T(8,128)(2,1)S(1)}, bf16[128,128]{1,0:T(8,128)(2,1)S(1)}, u32[]{:S(2)}, u32[]{:S(2)}) %collective-permute-start.2) | collective-permute-done | bytes 32800 | tf_op jit(solution)/shard_map/while/body/eval_jaxpr/ppermute | solution.py:12
  93.1 6.8 %collective-permute-done.3 = bf16[256,128]{1,0:T(8,128)(2,1)S(1)} collective-permute-done((bf16[256,128]{1,0:T(8,128)(2,1)S(1)}, bf16[256,128]{1,0:T(8,128)(2,1)S(1)}, u32[]{:S(2)}, u32[]{:S(2)}) %collective-permute-start.3) | collective-permute-done | bytes 65568 | tf_op jit(solution)/shard_map/while/body/eval_jaxpr/ppermute | solution.py:12
  104.2 5.8 %collective-permute-done.4 = bf16[256,128]{1,0:T(8,128)(2,1)S(1)} collective-permute-done((bf16[256,128]{1,0:T(8,128)(2,1)S(1)}, bf16[256,128]{1,0:T(8,128)(2,1)S(1)}, u32[]{:S(2)}, u32[]{:S(2)}) %collective-permute-start.4) | collective-permute-done | bytes 65568 | tf_op jit(solution)/shard_map/while/body/eval_jaxpr/ppermute | solution.py:12
  142.3 6.0 %collective-permute-done.2 = bf16[128,128]{1,0:T(8,128)(2,1)S(1)} collective-permute-done((bf16[128,128]{1,0:T(8,128)(2,1)S(1)}, bf16[128,128]{1,0:T(8,128)(2,1)S(1)}, u32[]{:S(2)}, u32[]{:S(2)}) %collective-permute-start.2) | collective-permute-done | bytes 32800 | tf_op jit(solution)/shard_map/while/body/eval_jaxpr/ppermute | solution.py:12
  150.7 6.8 %collective-permute-done.3 = bf16[256,128]{1,0:T(8,128)(2,1)S(1)} collective-permute-done((bf16[256,128]{1,0:T(8,128)(2,1)S(1)}, bf16[256,128]{1,0:T(8,128)(2,1)S(1)}, u32[]{:S(2)}, u32[]{:S(2)}) %collective-permute-start.3) | collective-permute-done | bytes 65568 | tf_op jit(solution)/shard_map/while/body/eval_jaxpr/ppermute | solution.py:12
  161.7 5.8 %collective-permute-done.4 = bf16[256,128]{1,0:T(8,128)(2,1)S(1)} collective-permute-done((bf16[256,128]{1,0:T(8,128)(2,1)S(1)}, bf16[256,128]{1,0:T(8,128)(2,1)S(1)}, u32[]{:S(2)}, u32[]{:S(2)}) %collective-permute-start.4) | collective-permute-done | bytes 65568 | tf_op jit(solution)/shard_map/while/body/eval_jaxpr/ppermute | solution.py:12
  200.1 6.0 %collective-permute-done.2 = bf16[128,128]{1,0:T(8,128)(2,1)S(1)} collective-permute-done((bf16[128,128]{1,0:T(8,128)(2,1)S(1)}, bf16[128,128]{1,0:T(8,128)(2,1)S(1)}, u32[]{:S(2)}, u32[]{:S(2)}) %collective-permute-start.2) | collective-permute-done | bytes 32800 | tf_op jit(solution)/shard_map/while/body/eval_jaxpr/ppermute | solution.py:12
  208.5 6.8 %collective-permute-done.3 = bf16[256,128]{1,0:T(8,128)(2,1)S(1)} collective-permute-done((bf16[256,128]{1,0:T(8,128)(2,1)S(1)}, bf16[256,128]{1,0:T(8,128)(2,1)S(1)}, u32[]{:S(2)}, u32[]{:S(2)}) %collective-permute-start.3) | collective-permute-done | bytes 65568 | tf_op jit(solution)/shard_map/while/body/eval_jaxpr/ppermute | solution.py:12
  219.6 5.7 %collective-permute-done.4 = bf16[256,128]{1,0:T(8,128)(2,1)S(1)} collective-permute-done((bf16[256,128]{1,0:T(8,128)(2,1)S(1)}, bf16[256,128]{1,0:T(8,128)(2,1)S(1)}, u32[]{:S(2)}, u32[]{:S(2)}) %collective-permute-start.4) | collective-permute-done | bytes 65568 | tf_op jit(solution)/shard_map/while/body/eval_jaxpr/ppermute | solution.py:12
  258.0 6.0 %collective-permute-done.2 = bf16[128,128]{1,0:T(8,128)(2,1)S(1)} collective-permute-done((bf16[128,128]{1,0:T(8,128)(2,1)S(1)}, bf16[128,128]{1,0:T(8,128)(2,1)S(1)}, u32[]{:S(2)}, u32[]{:S(2)}) %collective-permute-start.2) | collective-permute-done | bytes 32800 | tf_op jit(solution)/shard_map/while/body/eval_jaxpr/ppermute | solution.py:12
  266.4 6.8 %collective-permute-done.3 = bf16[256,128]{1,0:T(8,128)(2,1)S(1)} collective-permute-done((bf16[256,128]{1,0:T(8,128)(2,1)S(1)}, bf16[256,128]{1,0:T(8,128)(2,1)S(1)}, u32[]{:S(2)}, u32[]{:S(2)}) %collective-permute-start.3) | collective-permute-done | bytes 65568 | tf_op jit(solution)/shard_map/while/body/eval_jaxpr/ppermute | solution.py:12
  315.8 6.0 %collective-permute-done.2 = bf16[128,128]{1,0:T(8,128)(2,1)S(1)} collective-permute-done((bf16[128,128]{1,0:T(8,128)(2,1)S(1)}, bf16[128,128]{1,0:T(8,128)(2,1)S(1)}, u32[]{:S(2)}, u32[]{:S(2)}) %collective-permute-start.2) | collective-permute-done | bytes 32800 | tf_op jit(solution)/shard_map/while/body/eval_jaxpr/ppermute | solution.py:12
  324.2 6.8 %collective-permute-done.3 = bf16[256,128]{1,0:T(8,128)(2,1)S(1)} collective-permute-done((bf16[256,128]{1,0:T(8,128)(2,1)S(1)}, bf16[256,128]{1,0:T(8,128)(2,1)S(1)}, u32[]{:S(2)}, u32[]{:S(2)}) %collective-permute-start.3) | collective-permute-done | bytes 65568 | tf_op jit(solution)/shard_map/while/body/eval_jaxpr/ppermute | solution.py:12
  373.7 6.0 %collective-permute-done.2 = bf16[128,128]{1,0:T(8,128)(2,1)S(1)} collective-permute-done((bf16[128,128]{1,0:T(8,128)(2,1)S(1)}, bf16[128,128]{1,0:T(8,128)(2,1)S(1)}, u32[]{:S(2)}, u32[]{:S(2)}) %collective-permute-start.2) | collective-permute-done | bytes 32800 | tf_op jit(solution)/shard_map/while/body/eval_jaxpr/ppermute | solution.py:12
  382.1 6.8 %collective-permute-done.3 = bf16[256,128]{1,0:T(8,128)(2,1)S(1)} collective-permute-done((bf16[256,128]{1,0:T(8,128)(2,1)S(1)}, bf16[256,128]{1,0:T(8,128)(2,1)S(1)}, u32[]{:S(2)}, u32[]{:S(2)}) %collective-permute-start.3) | collective-permute-done | bytes 65568 | tf_op jit(solution)/shard_map/while/body/eval_jaxpr/ppermute | solution.py:12
  431.6 6.0 %collective-permute-done.2 = bf16[128,128]{1,0:T(8,128)(2,1)S(1)} collective-permute-done((bf16[128,128]{1,0:T(8,128)(2,1)S(1)}, bf16[128,128]{1,0:T(8,128)(2,1)S(1)}, u32[]{:S(2)}, u32[]{:S(2)}) %collective-permute-start.2) | collective-permute-done | bytes 32800 | tf_op jit(solution)/shard_map/while/body/eval_jaxpr/ppermute | solution.py:12
  439.9 6.8 %collective-permute-done.3 = bf16[256,128]{1,0:T(8,128)(2,1)S(1)} collective-permute-done((bf16[256,128]{1,0:T(8,128)(2,1)S(1)}, bf16[256,128]{1,0:T(8,128)(2,1)S(1)}, u32[]{:S(2)}, u32[]{:S(2)}) %collective-permute-start.3) | collective-permute-done | bytes 65568 | tf_op jit(solution)/shard_map/while/body/eval_jaxpr/ppermute | solution.py:12
  489.4 6.0 %collective-permute-done.2 = bf16[128,128]{1,0:T(8,128)(2,1)S(1)} collective-permute-done((bf16[128,128]{1,0:T(8,128)(2,1)S(1)}, bf16[128,128]{1,0:T(8,128)(2,1)S(1)}, u32[]{:S(2)}, u32[]{:S(2)}) %collective-permute-start.2) | collective-permute-done | bytes 32800 | tf_op jit(solution)/shard_map/while/body/eval_jaxpr/ppermute | solution.py:12
  497.8 6.8 %collective-permute-done.3 = bf16[256,128]{1,0:T(8,128)(2,1)S(1)} collective-permute-done((bf16[256,128]{1,0:T(8,128)(2,1)S(1)}, bf16[256,128]{1,0:T(8,128)(2,1)S(1)}, u32[]{:S(2)}, u32[]{:S(2)}) %collective-permute-start.3) | collective-permute-done | bytes 65568 | tf_op jit(solution)/shard_map/while/body/eval_jaxpr/ppermute | solution.py:12
  (390 shorter events, 372.9 us)
Async XLA Ops:
  2.8 13.1 %collective-permute-start = (bf16[2,128]{1,0:T(2,128)(2,1)S(1)}, bf16[2,128]{1,0:T(2,128)(2,1)S(1)}, u32[]{:S(2)}, u32[]{:S(2)}) collective-permute-start(bf16[2,128]{1,0:T(2,128)(2,1)S(1)} %slice.556), channel_id=1, source_target_pairs={{0,1},{1,2},{2,3},{3,4},{4,5},{5,6},{6,7},{7,8},{8,9},{9,10},{10,1... | collective-permute-start | bytes 1544 | tf_op jit(solution)/shard_map/while/body/eval_jaxpr/ppermute | solution.py:12
  42.7 9.9 %collective-permute-start.4 = (bf16[256,128]{1,0:T(8,128)(2,1)S(1)}, bf16[256,128]{1,0:T(8,128)(2,1)S(1)}, u32[]{:S(2)}, u32[]{:S(2)}) collective-permute-start(bf16[256,128]{1,0:T(8,128)(2,1)S(1)} %fusion.164), channel_id=1, source_target_pairs={{0,2},{1,3},{2,4},{3,5},{4,6},{5,7},{6,8},{7,9},{8,10},{9,11},{10,... | collective-permute-start | bytes 196616 | tf_op jit(solution)/shard_map/while/body/eval_jaxpr/ppermute | solution.py:12
  44.6 11.8 %collective-permute-start.5 = (bf16[256,128]{1,0:T(8,128)(2,1)S(1)}, bf16[256,128]{1,0:T(8,128)(2,1)S(1)}, u32[]{:S(2)}, u32[]{:S(2)}) collective-permute-start(bf16[256,128]{1,0:T(8,128)(2,1)S(1)} %fusion.164), channel_id=1, source_target_pairs={{0,4},{1,5},{2,6},{3,7},{4,8},{5,9},{6,10},{7,11},{8,12},{9,13},{1... | collective-permute-start | bytes 196616 | tf_op jit(solution)/shard_map/while/body/eval_jaxpr/ppermute | solution.py:12
  100.3 9.6 %collective-permute-start.4 = (bf16[256,128]{1,0:T(8,128)(2,1)S(1)}, bf16[256,128]{1,0:T(8,128)(2,1)S(1)}, u32[]{:S(2)}, u32[]{:S(2)}) collective-permute-start(bf16[256,128]{1,0:T(8,128)(2,1)S(1)} %fusion.164), channel_id=1, source_target_pairs={{0,2},{1,3},{2,4},{3,5},{4,6},{5,7},{6,8},{7,9},{8,10},{9,11},{10,... | collective-permute-start | bytes 196616 | tf_op jit(solution)/shard_map/while/body/eval_jaxpr/ppermute | solution.py:12
  102.3 11.7 %collective-permute-start.5 = (bf16[256,128]{1,0:T(8,128)(2,1)S(1)}, bf16[256,128]{1,0:T(8,128)(2,1)S(1)}, u32[]{:S(2)}, u32[]{:S(2)}) collective-permute-start(bf16[256,128]{1,0:T(8,128)(2,1)S(1)} %fusion.164), channel_id=1, source_target_pairs={{0,4},{1,5},{2,6},{3,7},{4,8},{5,9},{6,10},{7,11},{8,12},{9,13},{1... | collective-permute-start | bytes 196616 | tf_op jit(solution)/shard_map/while/body/eval_jaxpr/ppermute | solution.py:12
  157.9 9.6 %collective-permute-start.4 = (bf16[256,128]{1,0:T(8,128)(2,1)S(1)}, bf16[256,128]{1,0:T(8,128)(2,1)S(1)}, u32[]{:S(2)}, u32[]{:S(2)}) collective-permute-start(bf16[256,128]{1,0:T(8,128)(2,1)S(1)} %fusion.164), channel_id=1, source_target_pairs={{0,2},{1,3},{2,4},{3,5},{4,6},{5,7},{6,8},{7,9},{8,10},{9,11},{10,... | collective-permute-start | bytes 196616 | tf_op jit(solution)/shard_map/while/body/eval_jaxpr/ppermute | solution.py:12
  159.8 12.0 %collective-permute-start.5 = (bf16[256,128]{1,0:T(8,128)(2,1)S(1)}, bf16[256,128]{1,0:T(8,128)(2,1)S(1)}, u32[]{:S(2)}, u32[]{:S(2)}) collective-permute-start(bf16[256,128]{1,0:T(8,128)(2,1)S(1)} %fusion.164), channel_id=1, source_target_pairs={{0,4},{1,5},{2,6},{3,7},{4,8},{5,9},{6,10},{7,11},{8,12},{9,13},{1... | collective-permute-start | bytes 196616 | tf_op jit(solution)/shard_map/while/body/eval_jaxpr/ppermute | solution.py:12
  206.6 8.7 %collective-permute-start.3 = (bf16[256,128]{1,0:T(8,128)(2,1)S(1)}, bf16[256,128]{1,0:T(8,128)(2,1)S(1)}, u32[]{:S(2)}, u32[]{:S(2)}) collective-permute-start(bf16[256,128]{1,0:T(8,128)(2,1)S(1)} %fusion.163), channel_id=1, source_target_pairs={{0,1},{1,2},{2,3},{3,4},{4,5},{5,6},{6,7},{7,8},{8,9},{9,10},{10,1... | collective-permute-start | bytes 196616 | tf_op jit(solution)/shard_map/while/body/eval_jaxpr/ppermute | solution.py:12
  215.7 9.6 %collective-permute-start.4 = (bf16[256,128]{1,0:T(8,128)(2,1)S(1)}, bf16[256,128]{1,0:T(8,128)(2,1)S(1)}, u32[]{:S(2)}, u32[]{:S(2)}) collective-permute-start(bf16[256,128]{1,0:T(8,128)(2,1)S(1)} %fusion.164), channel_id=1, source_target_pairs={{0,2},{1,3},{2,4},{3,5},{4,6},{5,7},{6,8},{7,9},{8,10},{9,11},{10,... | collective-permute-start | bytes 196616 | tf_op jit(solution)/shard_map/while/body/eval_jaxpr/ppermute | solution.py:12
  217.7 12.0 %collective-permute-start.5 = (bf16[256,128]{1,0:T(8,128)(2,1)S(1)}, bf16[256,128]{1,0:T(8,128)(2,1)S(1)}, u32[]{:S(2)}, u32[]{:S(2)}) collective-permute-start(bf16[256,128]{1,0:T(8,128)(2,1)S(1)} %fusion.164), channel_id=1, source_target_pairs={{0,4},{1,5},{2,6},{3,7},{4,8},{5,9},{6,10},{7,11},{8,12},{9,13},{1... | collective-permute-start | bytes 196616 | tf_op jit(solution)/shard_map/while/body/eval_jaxpr/ppermute | solution.py:12
  264.4 8.7 %collective-permute-start.3 = (bf16[256,128]{1,0:T(8,128)(2,1)S(1)}, bf16[256,128]{1,0:T(8,128)(2,1)S(1)}, u32[]{:S(2)}, u32[]{:S(2)}) collective-permute-start(bf16[256,128]{1,0:T(8,128)(2,1)S(1)} %fusion.163), channel_id=1, source_target_pairs={{0,1},{1,2},{2,3},{3,4},{4,5},{5,6},{6,7},{7,8},{8,9},{9,10},{10,1... | collective-permute-start | bytes 196616 | tf_op jit(solution)/shard_map/while/body/eval_jaxpr/ppermute | solution.py:12
  273.6 9.6 %collective-permute-start.4 = (bf16[256,128]{1,0:T(8,128)(2,1)S(1)}, bf16[256,128]{1,0:T(8,128)(2,1)S(1)}, u32[]{:S(2)}, u32[]{:S(2)}) collective-permute-start(bf16[256,128]{1,0:T(8,128)(2,1)S(1)} %fusion.164), channel_id=1, source_target_pairs={{0,2},{1,3},{2,4},{3,5},{4,6},{5,7},{6,8},{7,9},{8,10},{9,11},{10,... | collective-permute-start | bytes 196616 | tf_op jit(solution)/shard_map/while/body/eval_jaxpr/ppermute | solution.py:12
  275.5 12.0 %collective-permute-start.5 = (bf16[256,128]{1,0:T(8,128)(2,1)S(1)}, bf16[256,128]{1,0:T(8,128)(2,1)S(1)}, u32[]{:S(2)}, u32[]{:S(2)}) collective-permute-start(bf16[256,128]{1,0:T(8,128)(2,1)S(1)} %fusion.164), channel_id=1, source_target_pairs={{0,4},{1,5},{2,6},{3,7},{4,8},{5,9},{6,10},{7,11},{8,12},{9,13},{1... | collective-permute-start | bytes 196616 | tf_op jit(solution)/shard_map/while/body/eval_jaxpr/ppermute | solution.py:12
  322.3 8.7 %collective-permute-start.3 = (bf16[256,128]{1,0:T(8,128)(2,1)S(1)}, bf16[256,128]{1,0:T(8,128)(2,1)S(1)}, u32[]{:S(2)}, u32[]{:S(2)}) collective-permute-start(bf16[256,128]{1,0:T(8,128)(2,1)S(1)} %fusion.163), channel_id=1, source_target_pairs={{0,1},{1,2},{2,3},{3,4},{4,5},{5,6},{6,7},{7,8},{8,9},{9,10},{10,1... | collective-permute-start | bytes 196616 | tf_op jit(solution)/shard_map/while/body/eval_jaxpr/ppermute | solution.py:12
  331.4 9.6 %collective-permute-start.4 = (bf16[256,128]{1,0:T(8,128)(2,1)S(1)}, bf16[256,128]{1,0:T(8,128)(2,1)S(1)}, u32[]{:S(2)}, u32[]{:S(2)}) collective-permute-start(bf16[256,128]{1,0:T(8,128)(2,1)S(1)} %fusion.164), channel_id=1, source_target_pairs={{0,2},{1,3},{2,4},{3,5},{4,6},{5,7},{6,8},{7,9},{8,10},{9,11},{10,... | collective-permute-start | bytes 196616 | tf_op jit(solution)/shard_map/while/body/eval_jaxpr/ppermute | solution.py:12
  333.4 12.0 %collective-permute-start.5 = (bf16[256,128]{1,0:T(8,128)(2,1)S(1)}, bf16[256,128]{1,0:T(8,128)(2,1)S(1)}, u32[]{:S(2)}, u32[]{:S(2)}) collective-permute-start(bf16[256,128]{1,0:T(8,128)(2,1)S(1)} %fusion.164), channel_id=1, source_target_pairs={{0,4},{1,5},{2,6},{3,7},{4,8},{5,9},{6,10},{7,11},{8,12},{9,13},{1... | collective-permute-start | bytes 196616 | tf_op jit(solution)/shard_map/while/body/eval_jaxpr/ppermute | solution.py:12
  380.1 8.7 %collective-permute-start.3 = (bf16[256,128]{1,0:T(8,128)(2,1)S(1)}, bf16[256,128]{1,0:T(8,128)(2,1)S(1)}, u32[]{:S(2)}, u32[]{:S(2)}) collective-permute-start(bf16[256,128]{1,0:T(8,128)(2,1)S(1)} %fusion.163), channel_id=1, source_target_pairs={{0,1},{1,2},{2,3},{3,4},{4,5},{5,6},{6,7},{7,8},{8,9},{9,10},{10,1... | collective-permute-start | bytes 196616 | tf_op jit(solution)/shard_map/while/body/eval_jaxpr/ppermute | solution.py:12
  389.3 9.6 %collective-permute-start.4 = (bf16[256,128]{1,0:T(8,128)(2,1)S(1)}, bf16[256,128]{1,0:T(8,128)(2,1)S(1)}, u32[]{:S(2)}, u32[]{:S(2)}) collective-permute-start(bf16[256,128]{1,0:T(8,128)(2,1)S(1)} %fusion.164), channel_id=1, source_target_pairs={{0,2},{1,3},{2,4},{3,5},{4,6},{5,7},{6,8},{7,9},{8,10},{9,11},{10,... | collective-permute-start | bytes 196616 | tf_op jit(solution)/shard_map/while/body/eval_jaxpr/ppermute | solution.py:12
  391.2 12.0 %collective-permute-start.5 = (bf16[256,128]{1,0:T(8,128)(2,1)S(1)}, bf16[256,128]{1,0:T(8,128)(2,1)S(1)}, u32[]{:S(2)}, u32[]{:S(2)}) collective-permute-start(bf16[256,128]{1,0:T(8,128)(2,1)S(1)} %fusion.164), channel_id=1, source_target_pairs={{0,4},{1,5},{2,6},{3,7},{4,8},{5,9},{6,10},{7,11},{8,12},{9,13},{1... | collective-permute-start | bytes 196616 | tf_op jit(solution)/shard_map/while/body/eval_jaxpr/ppermute | solution.py:12
  447.1 9.6 %collective-permute-start.4 = (bf16[256,128]{1,0:T(8,128)(2,1)S(1)}, bf16[256,128]{1,0:T(8,128)(2,1)S(1)}, u32[]{:S(2)}, u32[]{:S(2)}) collective-permute-start(bf16[256,128]{1,0:T(8,128)(2,1)S(1)} %fusion.164), channel_id=1, source_target_pairs={{0,2},{1,3},{2,4},{3,5},{4,6},{5,7},{6,8},{7,9},{8,10},{9,11},{10,... | collective-permute-start | bytes 196616 | tf_op jit(solution)/shard_map/while/body/eval_jaxpr/ppermute | solution.py:12
  449.1 12.0 %collective-permute-start.5 = (bf16[256,128]{1,0:T(8,128)(2,1)S(1)}, bf16[256,128]{1,0:T(8,128)(2,1)S(1)}, u32[]{:S(2)}, u32[]{:S(2)}) collective-permute-start(bf16[256,128]{1,0:T(8,128)(2,1)S(1)} %fusion.164), channel_id=1, source_target_pairs={{0,4},{1,5},{2,6},{3,7},{4,8},{5,9},{6,10},{7,11},{8,12},{9,13},{1... | collective-permute-start | bytes 196616 | tf_op jit(solution)/shard_map/while/body/eval_jaxpr/ppermute | solution.py:12
  495.9 8.7 %collective-permute-start.3 = (bf16[256,128]{1,0:T(8,128)(2,1)S(1)}, bf16[256,128]{1,0:T(8,128)(2,1)S(1)}, u32[]{:S(2)}, u32[]{:S(2)}) collective-permute-start(bf16[256,128]{1,0:T(8,128)(2,1)S(1)} %fusion.163), channel_id=1, source_target_pairs={{0,1},{1,2},{2,3},{3,4},{4,5},{5,6},{6,7},{7,8},{8,9},{9,10},{10,1... | collective-permute-start | bytes 196616 | tf_op jit(solution)/shard_map/while/body/eval_jaxpr/ppermute | solution.py:12
  505.0 9.6 %collective-permute-start.4 = (bf16[256,128]{1,0:T(8,128)(2,1)S(1)}, bf16[256,128]{1,0:T(8,128)(2,1)S(1)}, u32[]{:S(2)}, u32[]{:S(2)}) collective-permute-start(bf16[256,128]{1,0:T(8,128)(2,1)S(1)} %fusion.164), channel_id=1, source_target_pairs={{0,2},{1,3},{2,4},{3,5},{4,6},{5,7},{6,8},{7,9},{8,10},{9,11},{10,... | collective-permute-start | bytes 196616 | tf_op jit(solution)/shard_map/while/body/eval_jaxpr/ppermute | solution.py:12
  506.9 12.0 %collective-permute-start.5 = (bf16[256,128]{1,0:T(8,128)(2,1)S(1)}, bf16[256,128]{1,0:T(8,128)(2,1)S(1)}, u32[]{:S(2)}, u32[]{:S(2)}) collective-permute-start(bf16[256,128]{1,0:T(8,128)(2,1)S(1)} %fusion.164), channel_id=1, source_target_pairs={{0,4},{1,5},{2,6},{3,7},{4,8},{5,9},{6,10},{7,11},{8,12},{9,13},{1... | collective-permute-start | bytes 196616 | tf_op jit(solution)/shard_map/while/body/eval_jaxpr/ppermute | solution.py:12
  (63 other events, 422.9 us)
where the time goes:
time: 530 us; the launch traced here: 528 us
  waiting for transfers between devices  342 us (65%)
  starting transfers between devices  140 us (26%)
  matrix products  27.7 us (5%)
  loops' own time  7.25 us (1%)
  local copies, waits for them, and re-layouts  7.17 us (1%)
    ppermute x72, waiting for transfers between devices, passed_along(): return lax.ppermute(x, axis, pairs)  342 us
    ppermute x72, starting transfers between devices, passed_along(): return lax.ppermute(x, axis, pairs)  140 us
    dot_general x45, matrix products, apply_layer(): jnp.dot(inputs, conv_weight[0, layer], preferred_element_type=jnp.float32)  19.1 us
  transfers between devices with their start and end apart: 72, of which 72 were waited for; matrix products, arithmetic and copies ran while one was open for 0% of the time, Pallas kernels for 0%

commit v1 on v0

v1 whole, which is shorter than its diff:
```python
import jax
import jax.numpy as jnp
from jax import lax
from jax.experimental import pallas as pl
from jax.experimental.pallas import tpu as pltpu
from jax.sharding import PartitionSpec as P

MESH = pl.DeviceIdType.MESH
C = 128
ROWS = 256
NB = 64
FAR = 176
HALO = FAR + ROWS
SPAN = HALO + ROWS
LAYERS = 5
SPANS = (1, 16, 64, 128, 512)
QUARTER = 64
CUT = 176
EARLY = (CUT, ROWS)
LATE = (0, CUT)
OWN = ((0, 16, ROWS), (1, 48, ROWS), (2, 176, ROWS))
NEAR = ((0, -240, 16), (1, -208, 48), (2, -80, 176), (3, 176, ROWS))
DISTANT = ((0, -416, -240), (1, -384, -208), (2, -256, -80), (3, 0, 176))


def kernel(signal, conv_w, conv_b, out_w, out_b, result,
           wc, wo, bc, bo, ha, h0f, hbuf, xb, xo, xback, hend, sk, skin, made, relay,
           wsend, wsem, a_send, a_sem, r_send, r_sem, init_send, b_send, b_sem, h_send, s_send, s_sem,
           o_send, o_sem, done):
    section = lax.axis_index("section")
    tm = lax.axis_index("tm")
    x, c = section // 2, section % 2
    y, z = tm // 16, tm % 16
    turned = (y + 3 + c) % 4
    pos = z * 4 + (turned ^ (turned >> 1))
    t = jnp.where(c == 1, pos, NB - 1 - pos)
    step = 2 * c - 1

    def tm_of(p, rec):
        n = p % 4
        return (((n ^ (n >> 1)) + 1 - rec) % 4) * 16 + p // 4

    def ahead(k):
        return tm_of((pos + step * k + NB) % NB, c)

    def worker(block, rec):
        return tm_of(jnp.where(rec == 1, block, NB - 1 - block), rec)

    other = 1 - c
    mine = jnp.where(tm == t, 1, 0)

    barrier = pltpu.get_barrier_semaphore()

    def greet(sec, where):
        pl.semaphore_signal(barrier, inc=1, device_id=(sec, where), device_id_type=MESH)

    greet(x * 2 + other, tm)
    for k in (1, 2, 4):
        greet(section, ahead(-k))

    @pl.when(x > 0)
    def _():
        for k in range(3):
            greet(section - 2, ahead(-k))

    greet(x * 2 + other, t)

    @pl.when(x == 0)
    def _():
        for plane in range(4):
            for k in range(3):
                if plane > 0 or k == 1:
                    greet(plane * 2 + c, ahead(-k))

    for m in range(2):
        @pl.when(jnp.logical_or(c != m, tm != worker(tm, m)))
        def _():
            greet(x * 2 + m, worker(tm, m))

    pl.semaphore_wait(barrier, 7 - mine + jnp.where(x < 3, 3, 0) + jnp.where(x == 0, 1, 3))

    def remote(src, dst, send, recv, sec, where):
        return pltpu.make_async_remote_copy(
            src_ref=src, dst_ref=dst, send_sem=send, recv_sem=recv,
            device_id=(sec, where), device_id_type=MESH)

    quarter = remote(signal.at[other, pl.ds(pl.multiple_of(x * QUARTER, QUARTER), QUARTER)], relay, r_send, r_sem,
                     x * 2 + other, worker(tm, other))
    quarter.start()

    parts = (
        ((EARLY, HALO), (LATE, HALO)),
        ((EARLY, FAR), (LATE, FAR)),
        ((EARLY, FAR - ROWS), ((ROWS - FAR, CUT), FAR - ROWS)),
    )

    def start_copies(g, src, sends, sec):
        out = []
        for k in range(3):
            for i, ((lo, hi), base) in enumerate(parts[k]):
                out.append(remote(src.at[pl.ds(lo, hi - lo)], ha.at[g, pl.ds(base + lo, hi - lo)],
                                  sends.at[k, i], a_sem.at[g, k, i if g else 0], sec, ahead(k)))
        return out

    jobs = []
    for layer in range(LAYERS):
        jobs.append((conv_w.at[0, layer], lambda g, l=layer: wc.at[g, l]))
        jobs.append((out_w.at[0, layer], lambda g, l=layer: wo.at[g, l]))
        if layer == 0:
            jobs.append((conv_b, lambda g: bc.at[g]))
            jobs.append((out_b, lambda g: bo.at[g]))
    w_copies = []
    for i, (src, dst) in enumerate(jobs):
        cp = remote(src, dst(c), wsend.at[i], wsem.at[c, i], x * 2 + other, tm)
        cp.start()
        w_copies.append(cp)
        pltpu.make_async_copy(src, dst(c), wsem.at[c, i]).start()
    need = {0: (0, 1, 2, 3), 1: (4, 5), 2: (6, 7), 3: (8, 9), 4: (10, 11)}

    def wait_weights(g, layer):
        for i in need[layer]:
            src, dst = jobs[i]
            pltpu.make_async_copy(src, dst(g), wsem.at[g, i]).wait()

    def dense(taps, g, layer, own):
        pre = jnp.dot(jnp.concatenate(taps, axis=1), wc[g, layer],
                      preferred_element_type=jnp.float32) + bc[g, layer]
        gated = (jnp.tanh(pre[:, :C]) * (0.5 * jnp.tanh(0.5 * pre[:, C:]) + 0.5)).astype(jnp.bfloat16)
        if own:
            return jnp.dot(gated, wo[g, layer], preferred_element_type=jnp.float32) + bo[g, layer]
        return (jnp.dot(gated, wo[g, layer, :, pl.ds(0, C)], preferred_element_type=jnp.float32)
                + bo[g, layer, :, pl.ds(0, C)])

    next_section = jnp.where(x < 3, section + 2, section - 6)
    hand = start_copies(0, hend, h_send, next_section)
    skip_hand = remote(made.at[1, 1], skin, s_send, s_sem, next_section, ahead(0))
    inner = start_copies(1, ha.at[1, pl.ds(HALO, ROWS)], a_send, section)
    b_copies = [[[remote(xo.at[g, pl.ds(lo, hi - lo)], xback.at[g, i, pl.ds(lo, hi - lo)],
                         b_send.at[g, i, j], b_sem.at[g, i, j], section, ahead(k))
                  for i, k in enumerate((2, 4))]
                 for j, (lo, hi) in enumerate((EARLY, LATE))] for g in range(2)]
    away = [jnp.logical_or(c != g, mine == 0) for g in range(2)]
    outs = [(remote(made.at[g], result.at[c], o_send.at[g], o_sem.at[c], x * 2 + g, t),
             pltpu.make_async_copy(made.at[g], result.at[c], o_sem.at[c])) for g in range(2)]

    def send_out(g):
        far, near = outs[g]

        @pl.when(away[g])
        def _():
            far.start()

        @pl.when(jnp.logical_not(away[g]))
        def _():
            near.start()

    def first_rows(k, row, n, start):
        base = (HALO, FAR, FAR - ROWS)[k]
        return remote(relay.at[pl.ds(row, n)], ha.at[0, pl.ds(pl.multiple_of(base + start, 16), n)],
                      init_send.at[k], a_sem.at[0, k, 0], c, ahead(k))

    first = x * QUARTER
    quarter.wait_recv()

    @pl.when(x == 0)
    def _():
        pltpu.make_async_copy(relay, ha.at[0, pl.ds(HALO, QUARTER)], a_sem.at[0, 0, 0]).start()
        first_rows(1, 0, QUARTER, 0).start()

    @pl.when(x > 0)
    def _():
        first_rows(0, 0, QUARTER, first).start()
        first_rows(1, 0, QUARTER, first).start()

    @pl.when(x == 1)
    def _():
        first_rows(2, 16, QUARTER - 16, QUARTER + 16).start()

    @pl.when(x > 1)
    def _():
        first_rows(2, 0, QUARTER, first).start()

    def wait_start(k):
        rows = (pl.ds(HALO, ROWS), pl.ds(FAR, ROWS), pl.ds(0, FAR))[k]
        pltpu.make_async_copy(ha.at[0, rows], ha.at[0, rows], a_sem.at[0, k, 0]).wait()

    seen1 = jnp.where(t >= 1, 1.0, 0.0).astype(jnp.float32)
    seen2 = jnp.where(t >= 2, 1.0, 0.0).astype(jnp.float32)

    def tasks(g, todo):
        for layer, first, last in todo:
            d = SPANS[layer]
            for lo, hi in ((first, last),):
                at, n = lo + HALO, hi - lo
                if layer == 0:
                    taps = [h0f[pl.ds(at - 2, n), :].astype(jnp.bfloat16),
                            h0f[pl.ds(at - 1, n), :].astype(jnp.bfloat16),
                            ha[g, pl.ds(at, n), :]]
                    before = h0f
                else:
                    src = xb.at[layer - 1]
                    taps = [src[pl.ds(at - 2 * d, n), :], src[pl.ds(at - d, n), :], src[pl.ds(at, n), :]]
                    before = hbuf
                post = dense(taps, g, layer, hi > 0)
                h = before[pl.ds(at, n), :] + post[:, :C]
                hbuf[pl.ds(at, n), :] = h
                for begin, end, seen in ((-HALO, -ROWS, seen2), (-ROWS, 0, seen1), (0, ROWS, None)):
                    i, j = max(begin, lo), min(end, hi)
                    if i >= j:
                        continue
                    part = h[i - lo:j - lo]
                    if seen is not None:
                        part = part * seen
                    else:
                        s = post[i - lo:j - lo, C:]
                        if layer > 0 or g > 0:
                            s = s + sk[pl.ds(i, j - i), :]
                        sk[pl.ds(i, j - i), :] = s
                    if layer < 3:
                        xb[layer, pl.ds(i + HALO, j - i), :] = part.astype(jnp.bfloat16)
                    else:
                        xo[g, pl.ds(i, j - i), :] = part.astype(jnp.bfloat16)

    def last_layer(g, j):
        lo, hi = (EARLY, LATE)[j]
        rows = pl.ds(lo, hi - lo)
        for cp in b_copies[g][j]:
            cp.wait_recv()

        @pl.when(t < 4)
        def _():
            xback[g, 1, rows] = jnp.zeros((hi - lo, C), jnp.bfloat16)

        @pl.when(t < 2)
        def _():
            xback[g, 0, rows] = jnp.zeros((hi - lo, C), jnp.bfloat16)

        post = dense([xback[g, 1, rows, :], xback[g, 0, rows, :], xo[g, rows, :]], g, 4, True)
        h = (hbuf[pl.ds(lo + HALO, hi - lo), :] + post[:, :C]).astype(jnp.bfloat16)
        if g == 0:
            ha[1, pl.ds(HALO + lo, hi - lo), :] = h
            for k in (1, 2):
                inner[2 * k + j].start()
        else:
            hend[rows, :] = h

            @pl.when(x < 3)
            def _():
                for k in range(3):
                    hand[2 * k + j].start()
        skip = sk[rows, :] + post[:, C:]
        sk[rows, :] = skip
        made[g, 0, rows, :] = h
        made[g, 1, rows, :] = skip.astype(jnp.bfloat16)

    def widen(g, lo, n):
        h0f[pl.ds(lo, n), :] = ha[g, pl.ds(lo, n), :].astype(jnp.float32)

    for g in range(2):
        def wait_halo(k):
            if g == 0:
                wait_start(k)
            else:
                for cp in inner[2 * k:2 * k + 2]:
                    cp.wait_recv()

        for layer in range(LAYERS - 1):
            wait_weights(g, layer)
        if g == 0:
            wait_start(0)
        widen(g, HALO, ROWS)
        tasks(g, OWN)

        wait_halo(1)

        @pl.when(t == 0)
        def _():
            ha[g, pl.ds(FAR, ROWS), :] = jnp.zeros((ROWS, C), jnp.bfloat16)

        widen(g, FAR, ROWS)
        tasks(g, NEAR)
        for cp in b_copies[g][0]:
            cp.start()
        wait_weights(g, 4)

        wait_halo(2)

        @pl.when(t < 2)
        def _():
            ha[g, pl.ds(0, FAR), :] = jnp.zeros((FAR, C), jnp.bfloat16)

        widen(g, 0, FAR)
        tasks(g, DISTANT)
        for cp in b_copies[g][1]:
            cp.start()
        if g == 0:
            @pl.when(x > 0)
            def _():
                skip_hand.wait_recv()
                sk[...] += skin[...].astype(jnp.float32)
        last_layer(g, 0)
        last_layer(g, 1)
        if g == 0:
            @pl.when(x == 3)
            def _():
                send_out(0)

    @pl.when(x < 3)
    def _():
        for cp in hand:
            cp.wait_send()
        skip_hand.start()
        skip_hand.wait_send()
        pl.semaphore_signal(done, inc=1, device_id=(x * 2 + other, tm), device_id_type=MESH)
        pl.semaphore_wait(done, 1)
        send_out(0)

    send_out(1)
    for m in range(2):
        pltpu.make_async_copy(made.at[0], result.at[m], o_sem.at[m]).wait()

    quarter.wait_send()

    @pl.when(x > 0)
    def _():
        first_rows(0, 0, QUARTER, first).wait_send()

    first_rows(1, 0, QUARTER, first).wait_send()

    @pl.when(x == 1)
    def _():
        first_rows(2, 16, QUARTER - 16, QUARTER + 16).wait_send()

    @pl.when(x > 1)
    def _():
        first_rows(2, 0, QUARTER, first).wait_send()

    for g in range(2):
        @pl.when(away[g])
        def _():
            outs[g][0].wait_send()

    for cp in w_copies:
        cp.wait_send()
    for cp in inner[2:]:
        cp.wait_send()
    for g in range(2):
        for cp in b_copies[g][0] + b_copies[g][1]:
            cp.wait_send()


def shards(signal, conv_weight, conv_bias, out_weight, out_bias):
    bf16, f32 = jnp.bfloat16, jnp.float32
    any_space = pl.BlockSpec(memory_space=pl.ANY)
    vmem = pl.BlockSpec(memory_space=pltpu.VMEM)
    dma = pltpu.SemaphoreType.DMA
    result = pl.pallas_call(
        kernel,
        out_shape=jax.ShapeDtypeStruct((2, 2, ROWS, C), bf16),
        in_specs=[any_space] * 5,
        out_specs=vmem,
        scratch_shapes=[
            pltpu.VMEM((2, LAYERS, 3 * C, 2 * C), bf16),
            pltpu.VMEM((2, LAYERS, C, 2 * C), bf16),
            pltpu.VMEM((2, LAYERS, 1, 2 * C), f32),
            pltpu.VMEM((2, LAYERS, 1, 2 * C), f32),
            pltpu.VMEM((2, SPAN, C), bf16),
            pltpu.VMEM((SPAN, C), f32),
            pltpu.VMEM((SPAN, C), f32),
            pltpu.VMEM((3, SPAN, C), bf16),
            pltpu.VMEM((2, ROWS, C), bf16),
            pltpu.VMEM((2, 2, ROWS, C), bf16),
            pltpu.VMEM((ROWS, C), bf16),
            pltpu.VMEM((ROWS, C), f32),
            pltpu.VMEM((ROWS, C), bf16),
            pltpu.VMEM((2, 2, ROWS, C), bf16),
            pltpu.VMEM((QUARTER, C), bf16),
            dma((12,)), dma((2, 12)),
            dma((3, 2)), dma((2, 3, 2)),
            dma, dma, dma((3,)),
            dma((2, 2, 2)), dma((2, 2, 2)),
            dma((3, 2)), dma, dma,
            dma((2,)), dma((2,)), pltpu.SemaphoreType.REGULAR,
        ],
        compiler_params=pltpu.CompilerParams(
            collective_id=0, has_side_effects=True, vmem_limit_bytes=63 * 1024 * 1024),
        cost_estimate=pl.CostEstimate(flops=2 * 2336 * 262144, bytes_accessed=4_000_000, transcendentals=2 * 2336 * 256),
    )(signal, conv_weight, conv_bias.reshape(LAYERS, 1, 2 * C), out_weight, out_bias.reshape(LAYERS, 1, 2 * C))
    return result[None, :, 0], result[None, :, 1].astype(f32)


def solution(mesh):
    return jax.shard_map(
        shards,
        mesh=mesh,
        in_specs=(
            P(None, "tm", None),
            P("section", None, None, None),
            P("section", None, None),
            P("section", None, None, None),
            P("section", None, None),
        ),
        out_specs=(P("section", None, "tm", None), P("section", None, "tm", None)),
        check_vma=False,
    )
```

time: 530 us -> 126 us (0.24)
  the two profiles are of different devices: /device:TPU:30 before, /device:TPU:15 now
where the time goes in v1:
time: 126 us
  Pallas kernels  123 us (98%)
  other arithmetic  1.75 us (1%)
    pallas_call x1, Pallas kernels, shards(): pl.pallas_call(kernel, out_shape=jax.ShapeDtypeStruct((2, 2, ROWS, C), bf...  123 us

profile of v1, /device:TPU:15, one launch (start us, length us, event | category | flops | bytes accessed | tf_op | source)
XLA Modules:
  0.0 125.7 jit_solution(9555046700282942320)
XLA Ops:
  0.6 123.4 %shard_map.68 = bf16[2,2,256,128]{3,2,1,0:T(8,128)(2,1)} custom-call(bf16[2,256,128]{2,1,0:T(8,128)(2,1)} %signal.1, bf16[1,5,384,256]{3,2,1,0:T(8,128)(2,1)} %conv_w.1, f32[5,1,256]{2,1,0:T(1,128)} %bitcast.7, bf16[1,5,128,256]{3,2,1,0:T(8,128)(2,1)} %out_w.1, f32[5,1,256]{2,1,0:T(1,128)} %bitcast.8), custom_call_target="tpu_custom_call" | custom-call | flops 1224736768 | bytes 4000000 | tf_op jit(solution)/shard_map/pallas_call | solution.py:357
  124.0 1.7 %bitcast_convert_fusion = (f32[1,2,256,128]{3,2,1,0:T(8,128)}, bf16[1,2,256,128]{3,2,1,0:T(8,128)(2,1)}) fusion(bf16[2,2,256,128]{3,2,1,0:T(8,128)(2,1)} %shard_map.68), kind=kLoop, calls=%fused_computation | loop fusion | flops 65536 | bytes 655360 | tf_op jit(solution)/shard_map/convert_element_type | solution.py:389

commit v2 on v1

--- a/solution.py
+++ b/solution.py
@@ -26,7 +26,7 @@
 def kernel(signal, conv_w, conv_b, out_w, out_b, result,
            wc, wo, bc, bo, ha, h0f, hbuf, xb, xo, xback, hend, sk, skin, made, relay,
            wsend, wsem, a_send, a_sem, r_send, r_sem, init_send, b_send, b_sem, h_send, s_send, s_sem,
-           o_send, o_sem, done):
+           o_send, o_sem, done, taken):
     section = lax.axis_index("section")
     tm = lax.axis_index("tm")
     x, c = section // 2, section % 2
@@ -125,7 +125,9 @@
     def dense(taps, g, layer, own):
         pre = jnp.dot(jnp.concatenate(taps, axis=1), wc[g, layer],
                       preferred_element_type=jnp.float32) + bc[g, layer]
-        gated = (jnp.tanh(pre[:, :C]) * (0.5 * jnp.tanh(0.5 * pre[:, C:]) + 0.5)).astype(jnp.bfloat16)
+        pre = pre.astype(jnp.bfloat16)
+        half = jnp.bfloat16(0.5)
+        gated = jnp.tanh(pre[:, :C]) * (half * jnp.tanh(half * pre[:, C:]) + half)
         if own:
             return jnp.dot(gated, wo[g, layer], preferred_element_type=jnp.float32) + bo[g, layer]
         return (jnp.dot(gated, wo[g, layer, :, pl.ds(0, C)], preferred_element_type=jnp.float32)
@@ -284,6 +286,10 @@
         wait_weights(g, 4)
 
         wait_halo(2)
+        if g == 0:
+            @pl.when(x > 0)
+            def _():
+                pl.semaphore_signal(taken, inc=1, device_id=(section - 2, tm), device_id_type=MESH)
 
         @pl.when(t < 2)
         def _():
@@ -311,6 +317,7 @@
             cp.wait_send()
         skip_hand.start()
         skip_hand.wait_send()
+        pl.semaphore_wait(taken, 1)
         pl.semaphore_signal(done, inc=1, device_id=(x * 2 + other, tm), device_id_type=MESH)
         pl.semaphore_wait(done, 1)
         send_out(0)
@@ -380,7 +387,8 @@
             dma, dma, dma((3,)),
             dma((2, 2, 2)), dma((2, 2, 2)),
             dma((3, 2)), dma, dma,
-            dma((2,)), dma((2,)), pltpu.SemaphoreType.REGULAR,
+            dma((2,)), dma((2,)),
+            pltpu.SemaphoreType.REGULAR, pltpu.SemaphoreType.REGULAR,
         ],
         compiler_params=pltpu.CompilerParams(
             collective_id=0, has_side_effects=True, vmem_limit_bytes=63 * 1024 * 1024),

time: 126 us -> 126 us (level)
  no operation moved by 1% of the time
where the time goes in v2:
time: 126 us
  Pallas kernels  123 us (98%)
  other arithmetic  1.75 us (1%)
    pallas_call x1, Pallas kernels, shards(): pl.pallas_call(kernel, out_shape=jax.ShapeDtypeStruct((2, 2, ROWS, C), bf...  123 us

profile of v2, /device:TPU:15, one launch (start us, length us, event | category | flops | bytes accessed | tf_op | source)
XLA Modules:
  0.0 125.8 jit_solution(8345933575459739751)
XLA Ops:
  0.6 123.4 %shard_map.68 = bf16[2,2,256,128]{3,2,1,0:T(8,128)(2,1)} custom-call(bf16[2,256,128]{2,1,0:T(8,128)(2,1)} %signal.1, bf16[1,5,384,256]{3,2,1,0:T(8,128)(2,1)} %conv_w.1, f32[5,1,256]{2,1,0:T(1,128)} %bitcast.7, bf16[1,5,128,256]{3,2,1,0:T(8,128)(2,1)} %out_w.1, f32[5,1,256]{2,1,0:T(1,128)} %bitcast.8), custom_call_target="tpu_custom_call" | custom-call | flops 1224736768 | bytes 4000000 | tf_op jit(solution)/shard_map/pallas_call | solution.py:364
  124.0 1.7 %bitcast_convert_fusion = (f32[1,2,256,128]{3,2,1,0:T(8,128)}, bf16[1,2,256,128]{3,2,1,0:T(8,128)(2,1)}) fusion(bf16[2,2,256,128]{3,2,1,0:T(8,128)(2,1)} %shard_map.68), kind=kLoop, calls=%fused_computation | loop fusion | flops 65536 | bytes 655360 | tf_op jit(solution)/shard_map/convert_element_type | solution.py:397

commit v3 on v2

--- a/solution.py
+++ b/solution.py
@@ -15,12 +15,15 @@
 LAYERS = 5
 SPANS = (1, 16, 64, 128, 512)
 QUARTER = 64
-CUT = 176
-EARLY = (CUT, ROWS)
-LATE = (0, CUT)
+CHUNK = 256
 OWN = ((0, 16, ROWS), (1, 48, ROWS), (2, 176, ROWS))
-NEAR = ((0, -240, 16), (1, -208, 48), (2, -80, 176), (3, 176, ROWS))
-DISTANT = ((0, -416, -240), (1, -384, -208), (2, -256, -80), (3, 0, 176))
+AFTER = ((0, -416, 16), (1, -384, 48), (2, -256, 176), (3, 0, ROWS))
+
+
+def pieces(lo, hi):
+    count = -(-(hi - lo) // CHUNK)
+    size = -(-(hi - lo) // (16 * count)) * 16
+    return [(at, min(at + size, hi)) for at in range(lo, hi, size)]
 
 
 def kernel(signal, conv_w, conv_b, out_w, out_b, result,
@@ -88,19 +91,11 @@
                      x * 2 + other, worker(tm, other))
     quarter.start()
 
-    parts = (
-        ((EARLY, HALO), (LATE, HALO)),
-        ((EARLY, FAR), (LATE, FAR)),
-        ((EARLY, FAR - ROWS), ((ROWS - FAR, CUT), FAR - ROWS)),
-    )
+    parts = ((0, ROWS, HALO), (0, ROWS, FAR), (ROWS - FAR, FAR, 0))
 
     def start_copies(g, src, sends, sec):
-        out = []
-        for k in range(3):
-            for i, ((lo, hi), base) in enumerate(parts[k]):
-                out.append(remote(src.at[pl.ds(lo, hi - lo)], ha.at[g, pl.ds(base + lo, hi - lo)],
-                                  sends.at[k, i], a_sem.at[g, k, i if g else 0], sec, ahead(k)))
-        return out
+        return [remote(src.at[pl.ds(lo, n)], ha.at[g, pl.ds(at, n)], sends.at[k], a_sem.at[g, k], sec, ahead(k))
+                for k, (lo, n, at) in enumerate(parts)]
 
     jobs = []
     for layer in range(LAYERS):
@@ -137,10 +132,8 @@
     hand = start_copies(0, hend, h_send, next_section)
     skip_hand = remote(made.at[1, 1], skin, s_send, s_sem, next_section, ahead(0))
     inner = start_copies(1, ha.at[1, pl.ds(HALO, ROWS)], a_send, section)
-    b_copies = [[[remote(xo.at[g, pl.ds(lo, hi - lo)], xback.at[g, i, pl.ds(lo, hi - lo)],
-                         b_send.at[g, i, j], b_sem.at[g, i, j], section, ahead(k))
-                  for i, k in enumerate((2, 4))]
-                 for j, (lo, hi) in enumerate((EARLY, LATE))] for g in range(2)]
+    b_copies = [[remote(xo.at[g], xback.at[g, i], b_send.at[g, i], b_sem.at[g, i], section, ahead(k))
+                 for i, k in enumerate((2, 4))] for g in range(2)]
     away = [jnp.logical_or(c != g, mine == 0) for g in range(2)]
     outs = [(remote(made.at[g], result.at[c], o_send.at[g], o_sem.at[c], x * 2 + g, t),
              pltpu.make_async_copy(made.at[g], result.at[c], o_sem.at[c])) for g in range(2)]
@@ -159,14 +152,14 @@
     def first_rows(k, row, n, start):
         base = (HALO, FAR, FAR - ROWS)[k]
         return remote(relay.at[pl.ds(row, n)], ha.at[0, pl.ds(pl.multiple_of(base + start, 16), n)],
-                      init_send.at[k], a_sem.at[0, k, 0], c, ahead(k))
+                      init_send.at[k], a_sem.at[0, k], c, ahead(k))
 
     first = x * QUARTER
     quarter.wait_recv()
 
     @pl.when(x == 0)
     def _():
-        pltpu.make_async_copy(relay, ha.at[0, pl.ds(HALO, QUARTER)], a_sem.at[0, 0, 0]).start()
+        pltpu.make_async_copy(relay, ha.at[0, pl.ds(HALO, QUARTER)], a_sem.at[0, 0]).start()
         first_rows(1, 0, QUARTER, 0).start()
 
     @pl.when(x > 0)
@@ -184,7 +177,7 @@
 
     def wait_start(k):
         rows = (pl.ds(HALO, ROWS), pl.ds(FAR, ROWS), pl.ds(0, FAR))[k]
-        pltpu.make_async_copy(ha.at[0, rows], ha.at[0, rows], a_sem.at[0, k, 0]).wait()
+        pltpu.make_async_copy(ha.at[0, rows], ha.at[0, rows], a_sem.at[0, k]).wait()
 
     seen1 = jnp.where(t >= 1, 1.0, 0.0).astype(jnp.float32)
     seen2 = jnp.where(t >= 2, 1.0, 0.0).astype(jnp.float32)
@@ -192,7 +185,7 @@
     def tasks(g, todo):
         for layer, first, last in todo:
             d = SPANS[layer]
-            for lo, hi in ((first, last),):
+            for lo, hi in pieces(first, last):
                 at, n = lo + HALO, hi - lo
                 if layer == 0:
                     taps = [h0f[pl.ds(at - 2, n), :].astype(jnp.bfloat16),
@@ -223,37 +216,38 @@
                     else:
                         xo[g, pl.ds(i, j - i), :] = part.astype(jnp.bfloat16)
 
-    def last_layer(g, j):
-        lo, hi = (EARLY, LATE)[j]
-        rows = pl.ds(lo, hi - lo)
-        for cp in b_copies[g][j]:
+    def last_layer(g):
+        for cp in b_copies[g]:
             cp.wait_recv()
 
         @pl.when(t < 4)
         def _():
-            xback[g, 1, rows] = jnp.zeros((hi - lo, C), jnp.bfloat16)
+            xback[g, 1] = jnp.zeros((ROWS, C), jnp.bfloat16)
 
         @pl.when(t < 2)
         def _():
-            xback[g, 0, rows] = jnp.zeros((hi - lo, C), jnp.bfloat16)
-
-        post = dense([xback[g, 1, rows, :], xback[g, 0, rows, :], xo[g, rows, :]], g, 4, True)
-        h = (hbuf[pl.ds(lo + HALO, hi - lo), :] + post[:, :C]).astype(jnp.bfloat16)
-        if g == 0:
-            ha[1, pl.ds(HALO + lo, hi - lo), :] = h
-            for k in (1, 2):
-                inner[2 * k + j].start()
+            xback[g, 0] = jnp.zeros((ROWS, C), jnp.bfloat16)
+
+        for lo, hi in pieces(0, ROWS):
+            rows = pl.ds(lo, hi - lo)
+            post = dense([xback[g, 1, rows, :], xback[g, 0, rows, :], xo[g, rows, :]], g, 4, True)
+            h = (hbuf[pl.ds(lo + HALO, hi - lo), :] + post[:, :C]).astype(jnp.bfloat16)
+            if g == 0:
+                ha[1, pl.ds(HALO + lo, hi - lo), :] = h
+            else:
+                hend[rows, :] = h
+            skip = sk[rows, :] + post[:, C:]
+            sk[rows, :] = skip
+            made[g, 0, rows, :] = h
+            made[g, 1, rows, :] = skip.astype(jnp.bfloat16)
+        if g == 0:
+            for cp in inner[1:]:
+                cp.start()
         else:
-            hend[rows, :] = h
-
             @pl.when(x < 3)
             def _():
-                for k in range(3):
-                    hand[2 * k + j].start()
-        skip = sk[rows, :] + post[:, C:]
-        sk[rows, :] = skip
-        made[g, 0, rows, :] = h
-        made[g, 1, rows, :] = skip.astype(jnp.bfloat16)
+                for cp in hand:
+                    cp.start()
 
     def widen(g, lo, n):
         h0f[pl.ds(lo, n), :] = ha[g, pl.ds(lo, n), :].astype(jnp.float32)
@@ -263,8 +257,7 @@
             if g == 0:
                 wait_start(k)
             else:
-                for cp in inner[2 * k:2 * k + 2]:
-                    cp.wait_recv()
+                inner[k].wait_recv()
 
         for layer in range(LAYERS - 1):
             wait_weights(g, layer)
@@ -274,38 +267,31 @@
         tasks(g, OWN)
 
         wait_halo(1)
-
-        @pl.when(t == 0)
-        def _():
-            ha[g, pl.ds(FAR, ROWS), :] = jnp.zeros((ROWS, C), jnp.bfloat16)
-
-        widen(g, FAR, ROWS)
-        tasks(g, NEAR)
-        for cp in b_copies[g][0]:
-            cp.start()
-        wait_weights(g, 4)
-
         wait_halo(2)
         if g == 0:
             @pl.when(x > 0)
             def _():
                 pl.semaphore_signal(taken, inc=1, device_id=(section - 2, tm), device_id_type=MESH)
 
-        @pl.when(t < 2)
+        @pl.when(t == 0)
+        def _():
+            ha[g, pl.ds(0, HALO), :] = jnp.zeros((HALO, C), jnp.bfloat16)
+
+        @pl.when(t == 1)
         def _():
             ha[g, pl.ds(0, FAR), :] = jnp.zeros((FAR, C), jnp.bfloat16)
 
-        widen(g, 0, FAR)
-        tasks(g, DISTANT)
-        for cp in b_copies[g][1]:
+        widen(g, 0, HALO)
+        tasks(g, AFTER)
+        for cp in b_copies[g]:
             cp.start()
+        wait_weights(g, 4)
         if g == 0:
             @pl.when(x > 0)
             def _():
                 skip_hand.wait_recv()
                 sk[...] += skin[...].astype(jnp.float32)
-        last_layer(g, 0)
-        last_layer(g, 1)
+        last_layer(g)
         if g == 0:
             @pl.when(x == 3)
             def _():
@@ -349,10 +335,10 @@
 
     for cp in w_copies:
         cp.wait_send()
-    for cp in inner[2:]:
+    for cp in inner[1:]:
         cp.wait_send()
     for g in range(2):
-        for cp in b_copies[g][0] + b_copies[g][1]:
+        for cp in b_copies[g]:
             cp.wait_send()
 
 
@@ -383,10 +369,10 @@
             pltpu.VMEM((2, 2, ROWS, C), bf16),
             pltpu.VMEM((QUARTER, C), bf16),
             dma((12,)), dma((2, 12)),
-            dma((3, 2)), dma((2, 3, 2)),
+            dma((3,)), dma((2, 3)),
             dma, dma, dma((3,)),
-            dma((2, 2, 2)), dma((2, 2, 2)),
-            dma((3, 2)), dma, dma,
+            dma((2, 2)), dma((2, 2)),
+            dma((3,)), dma, dma,
             dma((2,)), dma((2,)),
             pltpu.SemaphoreType.REGULAR, pltpu.SemaphoreType.REGULAR,
         ],

time: 126 us -> 125 us (level)
  the two profiles are of different devices: /device:TPU:15 before, /device:TPU:79 now
where the time goes in v3:
time: 125 us
  Pallas kernels  122 us (98%)
  other arithmetic  1.75 us (1%)
    pallas_call x1, Pallas kernels, shards(): pl.pallas_call(kernel, out_shape=jax.ShapeDtypeStruct((2, 2, ROWS, C), bf...  122 us

profile of v3, /device:TPU:79, one launch (start us, length us, event | category | flops | bytes accessed | tf_op | source)
XLA Modules:
  0.0 124.8 jit_solution(15191661314997160010)
XLA Ops:
  0.6 122.4 %shard_map.68 = bf16[2,2,256,128]{3,2,1,0:T(8,128)(2,1)} custom-call(bf16[2,256,128]{2,1,0:T(8,128)(2,1)} %signal.1, bf16[1,5,384,256]{3,2,1,0:T(8,128)(2,1)} %conv_w.1, f32[5,1,256]{2,1,0:T(1,128)} %bitcast.7, bf16[1,5,128,256]{3,2,1,0:T(8,128)(2,1)} %out_w.1, f32[5,1,256]{2,1,0:T(1,128)} %bitcast.8), custom_call_target="tpu_custom_call" | custom-call | flops 1224736768 | bytes 4000000 | tf_op jit(solution)/shard_map/pallas_call | solution.py:350
  123.0 1.7 %bitcast_convert_fusion = (f32[1,2,256,128]{3,2,1,0:T(8,128)}, bf16[1,2,256,128]{3,2,1,0:T(8,128)(2,1)}) fusion(bf16[2,2,256,128]{3,2,1,0:T(8,128)(2,1)} %shard_map.68), kind=kLoop, calls=%fused_computation | loop fusion | flops 65536 | bytes 655360 | tf_op jit(solution)/shard_map/convert_element_type | solution.py:383

commit v4 on v3

--- a/solution.py
+++ b/solution.py
@@ -34,20 +34,20 @@
     tm = lax.axis_index("tm")
     x, c = section // 2, section % 2
     y, z = tm // 16, tm % 16
-    turned = (y + 3 + c) % 4
+    turned = (y + 4 - c) % 4
     pos = z * 4 + (turned ^ (turned >> 1))
-    t = jnp.where(c == 1, pos, NB - 1 - pos)
-    step = 2 * c - 1
+    t = jnp.where(c == 0, pos, NB - 1 - pos)
+    step = 1 - 2 * c
 
     def tm_of(p, rec):
         n = p % 4
-        return (((n ^ (n >> 1)) + 1 - rec) % 4) * 16 + p // 4
+        return (((n ^ (n >> 1)) + rec) % 4) * 16 + p // 4
 
     def ahead(k):
         return tm_of((pos + step * k + NB) % NB, c)
 
     def worker(block, rec):
-        return tm_of(jnp.where(rec == 1, block, NB - 1 - block), rec)
+        return tm_of(jnp.where(rec == 0, block, NB - 1 - block), rec)
 
     other = 1 - c
     mine = jnp.where(tm == t, 1, 0)

time: 125 us -> 131 us (1.048)
  the two profiles are of different devices: /device:TPU:79 before, /device:TPU:23 now
where the time goes in v4:
time: 131 us
  Pallas kernels  128 us (98%)
  other arithmetic  1.75 us (1%)
    pallas_call x1, Pallas kernels, shards(): pl.pallas_call(kernel, out_shape=jax.ShapeDtypeStruct((2, 2, ROWS, C), bf...  128 us

profile of v4, /device:TPU:23, one launch (start us, length us, event | category | flops | bytes accessed | tf_op | source)
XLA Modules:
  0.0 130.6 jit_solution(680936945257540227)
XLA Ops:
  0.6 128.2 %shard_map.68 = bf16[2,2,256,128]{3,2,1,0:T(8,128)(2,1)} custom-call(bf16[2,256,128]{2,1,0:T(8,128)(2,1)} %signal.1, bf16[1,5,384,256]{3,2,1,0:T(8,128)(2,1)} %conv_w.1, f32[5,1,256]{2,1,0:T(1,128)} %bitcast.7, bf16[1,5,128,256]{3,2,1,0:T(8,128)(2,1)} %out_w.1, f32[5,1,256]{2,1,0:T(1,128)} %bitcast.8), custom_call_target="tpu_custom_call" | custom-call | flops 1224736768 | bytes 4000000 | tf_op jit(solution)/shard_map/pallas_call | solution.py:350
  128.9 1.7 %bitcast_convert_fusion = (f32[1,2,256,128]{3,2,1,0:T(8,128)}, bf16[1,2,256,128]{3,2,1,0:T(8,128)(2,1)}) fusion(bf16[2,2,256,128]{3,2,1,0:T(8,128)(2,1)} %shard_map.68), kind=kLoop, calls=%fused_computation | loop fusion | flops 65536 | bytes 655360 | tf_op jit(solution)/shard_map/convert_element_type | solution.py:383

commit v5 on v3

--- a/solution.py
+++ b/solution.py
@@ -27,9 +27,9 @@
 
 
 def kernel(signal, conv_w, conv_b, out_w, out_b, result,
-           wc, wo, bc, bo, ha, h0f, hbuf, xb, xo, xback, hend, sk, skin, made, relay,
+           wc, wo, bc, bo, ha, h0f, hbuf, xb, xo, xback, hend, sk, skin, made, relay, via,
            wsend, wsem, a_send, a_sem, r_send, r_sem, init_send, b_send, b_sem, h_send, s_send, s_sem,
-           o_send, o_sem, done, taken):
+           o_send, o_sem, v_send, v_sem, done, taken):
     section = lax.axis_index("section")
     tm = lax.axis_index("tm")
     x, c = section // 2, section % 2
@@ -75,12 +75,21 @@
                 if plane > 0 or k == 1:
                     greet(plane * 2 + c, ahead(-k))
 
+    by_way = jnp.logical_and(x == 3, c == 0)
     for m in range(2):
-        @pl.when(jnp.logical_or(c != m, tm != worker(tm, m)))
+        @pl.when(jnp.logical_and(jnp.logical_not(by_way), jnp.logical_or(c != m, tm != worker(tm, m))))
         def _():
             greet(x * 2 + m, worker(tm, m))
 
-    pl.semaphore_wait(barrier, 7 - mine + jnp.where(x < 3, 3, 0) + jnp.where(x == 0, 1, 3))
+        @pl.when(by_way)
+        def _():
+            greet(m, tm)
+
+    @pl.when(x == 0)
+    def _():
+        greet(6 + c, worker(tm, c))
+
+    pl.semaphore_wait(barrier, 7 - jnp.where(by_way, 0, mine) + jnp.where(x < 3, 3, 0) + jnp.where(x == 0, 2, 3))
 
     def remote(src, dst, send, recv, sec, where):
         return pltpu.make_async_remote_copy(
@@ -137,6 +146,9 @@
     away = [jnp.logical_or(c != g, mine == 0) for g in range(2)]
     outs = [(remote(made.at[g], result.at[c], o_send.at[g], o_sem.at[c], x * 2 + g, t),
              pltpu.make_async_copy(made.at[g], result.at[c], o_sem.at[c])) for g in range(2)]
+
+    to_way = remote(made.at[0], via, o_send.at[0], v_sem, c, t)
+    from_way = remote(via, result.at[c], v_send, o_sem.at[c], 6, tm)
 
     def send_out(g):
         far, near = outs[g]
@@ -295,7 +307,7 @@
         if g == 0:
             @pl.when(x == 3)
             def _():
-                send_out(0)
+                to_way.start()
 
     @pl.when(x < 3)
     def _():
@@ -312,6 +324,16 @@
     for m in range(2):
         pltpu.make_async_copy(made.at[0], result.at[m], o_sem.at[m]).wait()
 
+    @pl.when(x == 0)
+    def _():
+        to_way.wait_recv()
+        from_way.start()
+        from_way.wait_send()
+
+    @pl.when(x == 3)
+    def _():
+        to_way.wait_send()
+
     quarter.wait_send()
 
     @pl.when(x > 0)
@@ -329,7 +351,7 @@
         first_rows(2, 0, QUARTER, first).wait_send()
 
     for g in range(2):
-        @pl.when(away[g])
+        @pl.when(jnp.logical_and(away[g], jnp.logical_or(x < 3, g == 1)))
         def _():
             outs[g][0].wait_send()
 
@@ -368,12 +390,13 @@
             pltpu.VMEM((ROWS, C), bf16),
             pltpu.VMEM((2, 2, ROWS, C), bf16),
             pltpu.VMEM((QUARTER, C), bf16),
+            pltpu.VMEM((2, ROWS, C), bf16),
             dma((12,)), dma((2, 12)),
             dma((3,)), dma((2, 3)),
             dma, dma, dma((3,)),
             dma((2, 2)), dma((2, 2)),
             dma((3,)), dma, dma,
-            dma((2,)), dma((2,)),
+            dma((2,)), dma((2,)), dma, dma,
             pltpu.SemaphoreType.REGULAR, pltpu.SemaphoreType.REGULAR,
         ],
         compiler_params=pltpu.CompilerParams(

time: 125 us -> 125 us (level)
  the two profiles are of different devices: /device:TPU:79 before, /device:TPU:15 now
where the time goes in v5:
time: 125 us
  Pallas kernels  122 us (98%)
  other arithmetic  1.75 us (1%)
    pallas_call x1, Pallas kernels, shards(): pl.pallas_call(kernel, out_shape=jax.ShapeDtypeStruct((2, 2, ROWS, C), bf...  122 us

profile of v5, /device:TPU:15, one launch (start us, length us, event | category | flops | bytes accessed | tf_op | source)
XLA Modules:
  0.0 124.7 jit_solution(1527343412879759232)
XLA Ops:
  0.6 122.3 %shard_map.68 = bf16[2,2,256,128]{3,2,1,0:T(8,128)(2,1)} custom-call(bf16[2,256,128]{2,1,0:T(8,128)(2,1)} %signal.1, bf16[1,5,384,256]{3,2,1,0:T(8,128)(2,1)} %conv_w.1, f32[5,1,256]{2,1,0:T(1,128)} %bitcast.7, bf16[1,5,128,256]{3,2,1,0:T(8,128)(2,1)} %out_w.1, f32[5,1,256]{2,1,0:T(1,128)} %bitcast.8), custom_call_target="tpu_custom_call" | custom-call | flops 1224736768 | bytes 4000000 | tf_op jit(solution)/shard_map/pallas_call | solution.py:372
  122.9 1.7 %bitcast_convert_fusion = (f32[1,2,256,128]{3,2,1,0:T(8,128)}, bf16[1,2,256,128]{3,2,1,0:T(8,128)(2,1)}) fusion(bf16[2,2,256,128]{3,2,1,0:T(8,128)(2,1)} %shard_map.68), kind=kLoop, calls=%fused_computation | loop fusion | flops 65536 | bytes 655360 | tf_op jit(solution)/shard_map/convert_element_type | solution.py:406

commit v6 on v3

--- a/solution.py
+++ b/solution.py
@@ -29,7 +29,7 @@
 def kernel(signal, conv_w, conv_b, out_w, out_b, result,
            wc, wo, bc, bo, ha, h0f, hbuf, xb, xo, xback, hend, sk, skin, made, relay,
            wsend, wsem, a_send, a_sem, r_send, r_sem, init_send, b_send, b_sem, h_send, s_send, s_sem,
-           o_send, o_sem, done, taken):
+           o_send, o_sem, done, taken, turn):
     section = lax.axis_index("section")
     tm = lax.axis_index("tm")
     x, c = section // 2, section % 2
@@ -157,6 +157,10 @@
     first = x * QUARTER
     quarter.wait_recv()
 
+    @pl.when(c == 1)
+    def _():
+        pl.semaphore_wait(turn, 1)
+
     @pl.when(x == 0)
     def _():
         pltpu.make_async_copy(relay, ha.at[0, pl.ds(HALO, QUARTER)], a_sem.at[0, 0]).start()
@@ -170,10 +174,22 @@
     @pl.when(x == 1)
     def _():
         first_rows(2, 16, QUARTER - 16, QUARTER + 16).start()
+        first_rows(2, 16, QUARTER - 16, QUARTER + 16).wait_send()
 
     @pl.when(x > 1)
     def _():
         first_rows(2, 0, QUARTER, first).start()
+        first_rows(2, 0, QUARTER, first).wait_send()
+
+    @pl.when(x > 0)
+    def _():
+        first_rows(0, 0, QUARTER, first).wait_send()
+
+    first_rows(1, 0, QUARTER, first).wait_send()
+
+    @pl.when(c == 0)
+    def _():
+        pl.semaphore_signal(turn, inc=1, device_id=(x * 2 + other, tm), device_id_type=MESH)
 
     def wait_start(k):
         rows = (pl.ds(HALO, ROWS), pl.ds(FAR, ROWS), pl.ds(0, FAR))[k]
@@ -314,20 +330,6 @@
 
     quarter.wait_send()
 
-    @pl.when(x > 0)
-    def _():
-        first_rows(0, 0, QUARTER, first).wait_send()
-
-    first_rows(1, 0, QUARTER, first).wait_send()
-
-    @pl.when(x == 1)
-    def _():
-        first_rows(2, 16, QUARTER - 16, QUARTER + 16).wait_send()
-
-    @pl.when(x > 1)
-    def _():
-        first_rows(2, 0, QUARTER, first).wait_send()
-
     for g in range(2):
         @pl.when(away[g])
         def _():
@@ -374,7 +376,7 @@
             dma((2, 2)), dma((2, 2)),
             dma((3,)), dma, dma,
             dma((2,)), dma((2,)),
-            pltpu.SemaphoreType.REGULAR, pltpu.SemaphoreType.REGULAR,
+            pltpu.SemaphoreType.REGULAR, pltpu.SemaphoreType.REGULAR, pltpu.SemaphoreType.REGULAR,
         ],
         compiler_params=pltpu.CompilerParams(
             collective_id=0, has_side_effects=True, vmem_limit_bytes=63 * 1024 * 1024),

time: 125 us -> 128 us (1.024)
  the two profiles are of different devices: /device:TPU:79 before, /device:TPU:15 now
where the time goes in v6:
time: 128 us
  Pallas kernels  125 us (98%)
  other arithmetic  1.75 us (1%)
    pallas_call x1, Pallas kernels, shards(): pl.pallas_call(kernel, out_shape=jax.ShapeDtypeStruct((2, 2, ROWS, C), bf...  125 us

profile of v6, /device:TPU:15, one launch (start us, length us, event | category | flops | bytes accessed | tf_op | source)
XLA Modules:
  0.0 127.5 jit_solution(5624121834009058114)
XLA Ops:
  0.6 125.1 %shard_map.68 = bf16[2,2,256,128]{3,2,1,0:T(8,128)(2,1)} custom-call(bf16[2,256,128]{2,1,0:T(8,128)(2,1)} %signal.1, bf16[1,5,384,256]{3,2,1,0:T(8,128)(2,1)} %conv_w.1, f32[5,1,256]{2,1,0:T(1,128)} %bitcast.7, bf16[1,5,128,256]{3,2,1,0:T(8,128)(2,1)} %out_w.1, f32[5,1,256]{2,1,0:T(1,128)} %bitcast.8), custom_call_target="tpu_custom_call" | custom-call | flops 1224736768 | bytes 4000000 | tf_op jit(solution)/shard_map/pallas_call | solution.py:352
  125.8 1.7 %bitcast_convert_fusion = (f32[1,2,256,128]{3,2,1,0:T(8,128)}, bf16[1,2,256,128]{3,2,1,0:T(8,128)(2,1)}) fusion(bf16[2,2,256,128]{3,2,1,0:T(8,128)(2,1)} %shard_map.68), kind=kLoop, calls=%fused_computation | loop fusion | flops 65536 | bytes 655360 | tf_op jit(solution)/shard_map/convert_element_type | solution.py:385

commit v7 on v3

--- a/solution.py
+++ b/solution.py
@@ -27,7 +27,7 @@
 
 
 def kernel(signal, conv_w, conv_b, out_w, out_b, result,
-           wc, wo, bc, bo, ha, h0f, hbuf, xb, xo, xback, hend, sk, skin, made, relay,
+           wc, wo, bc, bo, ha, h0f, hbuf, xb, xo, xback, hend, sk, gs, skin, made, relay,
            wsend, wsem, a_send, a_sem, r_send, r_sem, init_send, b_send, b_sem, h_send, s_send, s_sem,
            o_send, o_sem, done, taken):
     section = lax.axis_index("section")
@@ -117,16 +117,23 @@
             src, dst = jobs[i]
             pltpu.make_async_copy(src, dst(g), wsem.at[g, i]).wait()
 
-    def dense(taps, g, layer, own):
+    def dense(taps, g, layer):
         pre = jnp.dot(jnp.concatenate(taps, axis=1), wc[g, layer],
                       preferred_element_type=jnp.float32) + bc[g, layer]
         pre = pre.astype(jnp.bfloat16)
         half = jnp.bfloat16(0.5)
         gated = jnp.tanh(pre[:, :C]) * (half * jnp.tanh(half * pre[:, C:]) + half)
-        if own:
-            return jnp.dot(gated, wo[g, layer], preferred_element_type=jnp.float32) + bo[g, layer]
-        return (jnp.dot(gated, wo[g, layer, :, pl.ds(0, C)], preferred_element_type=jnp.float32)
-                + bo[g, layer, :, pl.ds(0, C)])
+        res = (jnp.dot(gated, wo[g, layer, :, pl.ds(0, C)], preferred_element_type=jnp.float32)
+               + bo[g, layer, :, pl.ds(0, C)])
+        return gated, res
+
+    def skip_part(g, layers):
+        weights = [wo[g, layer, :, pl.ds(C, C)] for layer in layers]
+        out = jnp.dot(jnp.concatenate([gs[layer] for layer in layers], axis=1), jnp.concatenate(weights, axis=0),
+                      preferred_element_type=jnp.float32)
+        for layer in layers:
+            out = out + bo[g, layer, :, pl.ds(C, C)]
+        return out
 
     next_section = jnp.where(x < 3, section + 2, section - 6)
     hand = start_copies(0, hend, h_send, next_section)
@@ -196,8 +203,8 @@
                     src = xb.at[layer - 1]
                     taps = [src[pl.ds(at - 2 * d, n), :], src[pl.ds(at - d, n), :], src[pl.ds(at, n), :]]
                     before = hbuf
-                post = dense(taps, g, layer, hi > 0)
-                h = before[pl.ds(at, n), :] + post[:, :C]
+                gated, res = dense(taps, g, layer)
+                h = before[pl.ds(at, n), :] + res
                 hbuf[pl.ds(at, n), :] = h
                 for begin, end, seen in ((-HALO, -ROWS, seen2), (-ROWS, 0, seen1), (0, ROWS, None)):
                     i, j = max(begin, lo), min(end, hi)
@@ -207,10 +214,7 @@
                     if seen is not None:
                         part = part * seen
                     else:
-                        s = post[i - lo:j - lo, C:]
-                        if layer > 0 or g > 0:
-                            s = s + sk[pl.ds(i, j - i), :]
-                        sk[pl.ds(i, j - i), :] = s
+                        gs[layer, pl.ds(i, j - i), :] = gated[i - lo:j - lo]
                     if layer < 3:
                         xb[layer, pl.ds(i + HALO, j - i), :] = part.astype(jnp.bfloat16)
                     else:
@@ -230,16 +234,13 @@
 
         for lo, hi in pieces(0, ROWS):
             rows = pl.ds(lo, hi - lo)
-            post = dense([xback[g, 1, rows, :], xback[g, 0, rows, :], xo[g, rows, :]], g, 4, True)
-            h = (hbuf[pl.ds(lo + HALO, hi - lo), :] + post[:, :C]).astype(jnp.bfloat16)
+            gated, res = dense([xback[g, 1, rows, :], xback[g, 0, rows, :], xo[g, rows, :]], g, 4)
+            h = (hbuf[pl.ds(lo + HALO, hi - lo), :] + res).astype(jnp.bfloat16)
+            gs[4, rows, :] = gated
             if g == 0:
                 ha[1, pl.ds(HALO + lo, hi - lo), :] = h
             else:
                 hend[rows, :] = h
-            skip = sk[rows, :] + post[:, C:]
-            sk[rows, :] = skip
-            made[g, 0, rows, :] = h
-            made[g, 1, rows, :] = skip.astype(jnp.bfloat16)
         if g == 0:
             for cp in inner[1:]:
                 cp.start()
@@ -249,6 +250,11 @@
                 for cp in hand:
                     cp.start()
 
+        skip = sk[...] + skip_part(g, (4,))
+        sk[...] = skip
+        made[g, 0] = ha[1, pl.ds(HALO, ROWS), :] if g == 0 else hend[...]
+        made[g, 1] = skip.astype(jnp.bfloat16)
+
     def widen(g, lo, n):
         h0f[pl.ds(lo, n), :] = ha[g, pl.ds(lo, n), :].astype(jnp.float32)
 
@@ -286,6 +292,10 @@
         for cp in b_copies[g]:
             cp.start()
         wait_weights(g, 4)
+        if g == 0:
+            sk[...] = skip_part(g, range(4))
+        else:
+            sk[...] += skip_part(g, range(4))
         if g == 0:
             @pl.when(x > 0)
             def _():
@@ -365,6 +375,7 @@
             pltpu.VMEM((2, 2, ROWS, C), bf16),
             pltpu.VMEM((ROWS, C), bf16),
             pltpu.VMEM((ROWS, C), f32),
+            pltpu.VMEM((LAYERS, ROWS, C), bf16),
             pltpu.VMEM((ROWS, C), bf16),
             pltpu.VMEM((2, 2, ROWS, C), bf16),
             pltpu.VMEM((QUARTER, C), bf16),

time: 125 us -> 125 us (level)
  no operation moved by 1% of the time
where the time goes in v7:
time: 125 us
  Pallas kernels  123 us (98%)
  other arithmetic  1.75 us (1%)
    pallas_call x1, Pallas kernels, shards(): pl.pallas_call(kernel, out_shape=jax.ShapeDtypeStruct((2, 2, ROWS, C), bf...  123 us

profile of v7, /device:TPU:79, one launch (start us, length us, event | category | flops | bytes accessed | tf_op | source)
XLA Modules:
  0.0 125.2 jit_solution(8723287586902870687)
XLA Ops:
  0.6 122.8 %shard_map.68 = bf16[2,2,256,128]{3,2,1,0:T(8,128)(2,1)} custom-call(bf16[2,256,128]{2,1,0:T(8,128)(2,1)} %signal.1, bf16[1,5,384,256]{3,2,1,0:T(8,128)(2,1)} %conv_w.1, f32[5,1,256]{2,1,0:T(1,128)} %bitcast.7, bf16[1,5,128,256]{3,2,1,0:T(8,128)(2,1)} %out_w.1, f32[5,1,256]{2,1,0:T(1,128)} %bitcast.8), custom_call_target="tpu_custom_call" | custom-call | flops 1224736768 | bytes 4000000 | tf_op jit(solution)/shard_map/pallas_call | solution.py:360
  123.5 1.7 %bitcast_convert_fusion = (f32[1,2,256,128]{3,2,1,0:T(8,128)}, bf16[1,2,256,128]{3,2,1,0:T(8,128)(2,1)}) fusion(bf16[2,2,256,128]{3,2,1,0:T(8,128)(2,1)} %shard_map.68), kind=kLoop, calls=%fused_computation | loop fusion | flops 65536 | bytes 655360 | tf_op jit(solution)/shard_map/convert_element_type | solution.py:394

commit v8 on v3

--- a/solution.py
+++ b/solution.py
@@ -14,7 +14,6 @@
 SPAN = HALO + ROWS
 LAYERS = 5
 SPANS = (1, 16, 64, 128, 512)
-QUARTER = 64
 CHUNK = 256
 OWN = ((0, 16, ROWS), (1, 48, ROWS), (2, 176, ROWS))
 AFTER = ((0, -416, 16), (1, -384, 48), (2, -256, 176), (3, 0, ROWS))
@@ -66,13 +65,15 @@
         for k in range(3):
             greet(section - 2, ahead(-k))
 
-    greet(x * 2 + other, t)
+    @pl.when(x != 2)
+    def _():
+        greet(x * 2 + other, t)
 
     @pl.when(x == 0)
     def _():
-        for plane in range(4):
+        for plane in (0, 1, 3):
             for k in range(3):
-                if plane > 0 or k == 1:
+                if plane > 0 or k > 0:
                     greet(plane * 2 + c, ahead(-k))
 
     for m in range(2):
@@ -80,16 +81,22 @@
         def _():
             greet(x * 2 + m, worker(tm, m))
 
-    pl.semaphore_wait(barrier, 7 - mine + jnp.where(x < 3, 3, 0) + jnp.where(x == 0, 1, 3))
+    pl.semaphore_wait(barrier, 6 - mine + jnp.where(x < 3, 3, 0) + jnp.where(x == 2, 0, jnp.where(x == 0, 3, 4)))
 
     def remote(src, dst, send, recv, sec, where):
         return pltpu.make_async_remote_copy(
             src_ref=src, dst_ref=dst, send_sem=send, recv_sem=recv,
             device_id=(sec, where), device_id_type=MESH)
 
-    quarter = remote(signal.at[other, pl.ds(pl.multiple_of(x * QUARTER, QUARTER), QUARTER)], relay, r_send, r_sem,
-                     x * 2 + other, worker(tm, other))
-    quarter.start()
+    def moved(start, n):
+        return remote(signal.at[other, pl.ds(start, n)], relay.at[pl.ds(0, n)], r_send, r_sem,
+                      x * 2 + other, worker(tm, other))
+
+    shares = ((0, 0, 128), (1, 128, 64), (3, 192, 64))
+    for plane, start, n in shares:
+        @pl.when(x == plane)
+        def _():
+            moved(start, n).start()
 
     parts = ((0, ROWS, HALO), (0, ROWS, FAR), (ROWS - FAR, FAR, 0))
 
@@ -151,29 +158,19 @@
 
     def first_rows(k, row, n, start):
         base = (HALO, FAR, FAR - ROWS)[k]
-        return remote(relay.at[pl.ds(row, n)], ha.at[0, pl.ds(pl.multiple_of(base + start, 16), n)],
+        return remote(relay.at[pl.ds(row, n)], ha.at[0, pl.ds(base + start, n)],
                       init_send.at[k], a_sem.at[0, k], c, ahead(k))
 
-    first = x * QUARTER
-    quarter.wait_recv()
-
-    @pl.when(x == 0)
-    def _():
-        pltpu.make_async_copy(relay, ha.at[0, pl.ds(HALO, QUARTER)], a_sem.at[0, 0]).start()
-        first_rows(1, 0, QUARTER, 0).start()
-
-    @pl.when(x > 0)
-    def _():
-        first_rows(0, 0, QUARTER, first).start()
-        first_rows(1, 0, QUARTER, first).start()
-
-    @pl.when(x == 1)
-    def _():
-        first_rows(2, 16, QUARTER - 16, QUARTER + 16).start()
-
-    @pl.when(x > 1)
-    def _():
-        first_rows(2, 0, QUARTER, first).start()
+    sends = {0: ((1, 0, 128, 0), (2, 80, 48, 80)), 1: [(k, 0, 64, 128) for k in range(3)],
+             3: [(k, 0, 64, 192) for k in range(3)]}
+    for plane, start, n in shares:
+        @pl.when(x == plane)
+        def _():
+            moved(start, n).wait_recv()
+            if plane == 0:
+                pltpu.make_async_copy(relay, ha.at[0, pl.ds(HALO, 128)], a_sem.at[0, 0]).start()
+            for args in sends[plane]:
+                first_rows(*args).start()
 
     def wait_start(k):
         rows = (pl.ds(HALO, ROWS), pl.ds(FAR, ROWS), pl.ds(0, FAR))[k]
@@ -312,21 +309,12 @@
     for m in range(2):
         pltpu.make_async_copy(made.at[0], result.at[m], o_sem.at[m]).wait()
 
-    quarter.wait_send()
-
-    @pl.when(x > 0)
-    def _():
-        first_rows(0, 0, QUARTER, first).wait_send()
-
-    first_rows(1, 0, QUARTER, first).wait_send()
-
-    @pl.when(x == 1)
-    def _():
-        first_rows(2, 16, QUARTER - 16, QUARTER + 16).wait_send()
-
-    @pl.when(x > 1)
-    def _():
-        first_rows(2, 0, QUARTER, first).wait_send()
+    for plane, start, n in shares:
+        @pl.when(x == plane)
+        def _():
+            moved(start, n).wait_send()
+            for args in sends[plane]:
+                first_rows(*args).wait_send()
 
     for g in range(2):
         @pl.when(away[g])
@@ -367,7 +355,7 @@
             pltpu.VMEM((ROWS, C), f32),
             pltpu.VMEM((ROWS, C), bf16),
             pltpu.VMEM((2, 2, ROWS, C), bf16),
-            pltpu.VMEM((QUARTER, C), bf16),
+            pltpu.VMEM((128, C), bf16),
             dma((12,)), dma((2, 12)),
             dma((3,)), dma((2, 3)),
             dma, dma, dma((3,)),

time: 125 us -> 125 us (level)
  the two profiles are of different devices: /device:TPU:79 before, /device:TPU:15 now
where the time goes in v8:
time: 125 us
  Pallas kernels  122 us (98%)
  other arithmetic  1.75 us (1%)
    pallas_call x1, Pallas kernels, shards(): pl.pallas_call(kernel, out_shape=jax.ShapeDtypeStruct((2, 2, ROWS, C), bf...  122 us

profile of v8, /device:TPU:15, one launch (start us, length us, event | category | flops | bytes accessed | tf_op | source)
XLA Modules:
  0.0 124.8 jit_solution(10357564223562332718)
XLA Ops:
  0.6 122.4 %shard_map.68 = bf16[2,2,256,128]{3,2,1,0:T(8,128)(2,1)} custom-call(bf16[2,256,128]{2,1,0:T(8,128)(2,1)} %signal.1, bf16[1,5,384,256]{3,2,1,0:T(8,128)(2,1)} %conv_w.1, f32[5,1,256]{2,1,0:T(1,128)} %bitcast.7, bf16[1,5,128,256]{3,2,1,0:T(8,128)(2,1)} %out_w.1, f32[5,1,256]{2,1,0:T(1,128)} %bitcast.8), custom_call_target="tpu_custom_call" | custom-call | flops 1224736768 | bytes 4000000 | tf_op jit(solution)/shard_map/pallas_call | solution.py:338
  123.0 1.7 %bitcast_convert_fusion = (f32[1,2,256,128]{3,2,1,0:T(8,128)}, bf16[1,2,256,128]{3,2,1,0:T(8,128)(2,1)}) fusion(bf16[2,2,256,128]{3,2,1,0:T(8,128)(2,1)} %shard_map.68), kind=kLoop, calls=%fused_computation | loop fusion | flops 65536 | bytes 655360 | tf_op jit(solution)/shard_map/convert_element_type | solution.py:371

commit v9 on v3

--- a/solution.py
+++ b/solution.py
@@ -272,6 +272,10 @@
             @pl.when(x > 0)
             def _():
                 pl.semaphore_signal(taken, inc=1, device_id=(section - 2, tm), device_id_type=MESH)
+        else:
+            @pl.when(x == 3)
+            def _():
+                send_out(0)
 
         @pl.when(t == 0)
         def _():
@@ -292,10 +296,6 @@
                 skip_hand.wait_recv()
                 sk[...] += skin[...].astype(jnp.float32)
         last_layer(g)
-        if g == 0:
-            @pl.when(x == 3)
-            def _():
-                send_out(0)
 
     @pl.when(x < 3)
     def _():

time: 125 us -> 126 us (level)
  the two profiles are of different devices: /device:TPU:79 before, /device:TPU:23 now
where the time goes in v9:
time: 126 us
  Pallas kernels  124 us (98%)
  other arithmetic  1.75 us (1%)
    pallas_call x1, Pallas kernels, shards(): pl.pallas_call(kernel, out_shape=jax.ShapeDtypeStruct((2, 2, ROWS, C), bf...  124 us

profile of v9, /device:TPU:23, one launch (start us, length us, event | category | flops | bytes accessed | tf_op | source)
XLA Modules:
  0.0 126.2 jit_solution(2207293123576441771)
XLA Ops:
  0.6 123.8 %shard_map.68 = bf16[2,2,256,128]{3,2,1,0:T(8,128)(2,1)} custom-call(bf16[2,256,128]{2,1,0:T(8,128)(2,1)} %signal.1, bf16[1,5,384,256]{3,2,1,0:T(8,128)(2,1)} %conv_w.1, f32[5,1,256]{2,1,0:T(1,128)} %bitcast.7, bf16[1,5,128,256]{3,2,1,0:T(8,128)(2,1)} %out_w.1, f32[5,1,256]{2,1,0:T(1,128)} %bitcast.8), custom_call_target="tpu_custom_call" | custom-call | flops 1224736768 | bytes 4000000 | tf_op jit(solution)/shard_map/pallas_call | solution.py:350
  124.4 1.7 %bitcast_convert_fusion = (f32[1,2,256,128]{3,2,1,0:T(8,128)}, bf16[1,2,256,128]{3,2,1,0:T(8,128)(2,1)}) fusion(bf16[2,2,256,128]{3,2,1,0:T(8,128)(2,1)} %shard_map.68), kind=kLoop, calls=%fused_computation | loop fusion | flops 65536 | bytes 655360 | tf_op jit(solution)/shard_map/convert_element_type | solution.py:383
